TPU v7x, 32 devices: a whole 2x2x4 slice. The times are simulated.
32 devices in a mesh: blk: 8 (over z, x), rep: 4 (over y, core).
Axes of the slice: x: 2, y: 2, z: 4, core: 2. Of those that a mesh axis runs over, the one named last changes fastest.
Arguments:
- features: bfloat16 [8192, 256], P(('blk', 'rep')), may hold values from -6 to 6
- weight: bfloat16 [256, 256], replicated, may hold values from -0.375 to 0.375
- pre_cot: bfloat16 [8192, 256], P(('blk', 'rep')), may hold values from -6 to 6
- tile_count: int32 [8, 4, 8], P('blk', 'rep'), may hold values from 0 to 2, as said below
- tile_rowid: int32 [8, 4, 8, 2], P('blk', 'rep'), may hold values from 0 to 3, as said below
- edge_cols: int32 [8, 4, 8, 2, 1, 256], P('blk', 'rep'), may hold values from 0 to 255
- edge_vals: bfloat16 [8, 4, 8, 2, 1, 256], P('blk', 'rep'), may hold values from -1.25 to 1.25
Outputs:
- activations: bfloat16 [8192, 256], P(('blk', 'rep'))
- grad_weight: float32 [256, 256], replicated
Inputs may be any that keep to these rules, and one draw needn't show every extreme that they name: `tile_count`: the panel p = b always has all 2 slots live. `tile_rowid`: the 2 slots of one block row, tile position and panel name distinct row tiles.
All inputs are finite; a program needn't handle non-finite values.
Results may differ from a plain program's by a relative error of at most 0.011.
Values may be sent and summed in bfloat16 or wider, within the bound.
A program may use at most 64 MiB of HBM per device.

v0:
```python
import jax
import jax.numpy as jnp
from jax import lax
from jax.sharding import PartitionSpec as P


def shifted(array, axis, by):
    count = lax.axis_size(axis)
    return lax.ppermute(array, axis, [(i, (i + by) % count) for i in range(count)])


def shards(features, weight, pre_cot, tile_count, tile_rowid, edge_cols, edge_vals):
    tile_rows = features.shape[0]
    feat_width = features.shape[1]
    rep_count = lax.axis_size("rep")
    blocks = lax.axis_size("blk")
    home_index = lax.axis_index("blk")
    counts = tile_count.reshape(-1)
    row_ids = tile_rowid.reshape(tile_rowid.shape[2], tile_rowid.shape[3])
    edge_index = edge_cols.reshape(edge_cols.shape[2:])
    edge_weight = edge_vals.reshape(edge_vals.shape[2:])
    slot_count = edge_index.shape[1]
    columns = lax.broadcasted_iota(jnp.int32, (1, 1, 1, tile_rows), 3)
    slot_ids = jnp.arange(slot_count, dtype=jnp.int32)
    zero_weight = jnp.zeros((), jnp.bfloat16)
    totals_start = jnp.zeros((rep_count * tile_rows, feat_width), jnp.float32)

    def apply_panel(totals, panel_now, panel_index):
        index_now = lax.dynamic_index_in_dim(edge_index, panel_index, 0, keepdims=False)
        weight_now = lax.dynamic_index_in_dim(edge_weight, panel_index, 0, keepdims=False)
        dense_tiles = jnp.sum(
            jnp.where(index_now[..., None] == columns, weight_now[..., None], zero_weight), axis=1
        )
        products = jnp.einsum(
            "sij,jf->sif", dense_tiles, panel_now, preferred_element_type=jnp.float32
        )
        live_mask = (slot_ids < counts[panel_index]).astype(jnp.float32)
        slot_rows = lax.dynamic_index_in_dim(row_ids, panel_index, 0, keepdims=False)
        for slot in range(slot_count):
            row_start = slot_rows[slot] * tile_rows
            current = lax.dynamic_slice_in_dim(totals, row_start, tile_rows, 0)
            totals = lax.dynamic_update_slice_in_dim(
                totals, current + products[slot] * live_mask[slot], row_start, 0
            )
        return totals

    totals = apply_panel(totals_start, features, home_index)

    def cycle_turn(turn_index, carry):
        totals_now, panel_now = carry
        panel_now = shifted(panel_now, "blk", 1)
        totals_now = apply_panel(totals_now, panel_now, (home_index - turn_index) % blocks)
        return (totals_now, panel_now)

    totals, _ = lax.fori_loop(1, blocks, cycle_turn, (totals, features))
    summed = lax.psum_scatter(totals.astype(jnp.bfloat16), "rep", scatter_dimension=0, tiled=True)
    preact = jnp.dot(summed, weight, preferred_element_type=jnp.float32)
    activations = jnp.maximum(preact, 0.0).astype(jnp.bfloat16)
    local_grad = lax.dot_general(
        summed, pre_cot, (((0,), (0,)), ((), ())), preferred_element_type=jnp.float32
    )
    total_grad = lax.psum(local_grad, ("blk", "rep"))
    node_total = blocks * rep_count * tile_rows
    grad_weight = total_grad * node_total ** (-0.5)
    return (activations, grad_weight)


def solution(mesh):
    in_specs = (
        P(("blk", "rep"), None),
        P(),
        P(("blk", "rep"), None),
        P("blk", "rep", None),
        P("blk", "rep", None, None),
        P("blk", "rep", None, None, None, None),
        P("blk", "rep", None, None, None, None),
    )
    out_specs = (P(("blk", "rep"), None), P())
    return jax.shard_map(shards, mesh=mesh, in_specs=in_specs, out_specs=out_specs, check_vma=False)
```

profile of v0, /device:TPU:0, one launch (start us, length us, event | category | flops | bytes accessed | tf_op | source)
XLA Modules:
  0.0 244.4 jit_solution(1695783370558010207)
XLA Ops:
  7.2 0.9 copy.30
  8.2 0.7 copy-done.3
  10.7 0.6 copy-done.5
  11.4 0.6 constant_dynamic-slice_fusion.3
  12.0 0.6 compare_convert_fusion.1
  12.6 0.6 fusion.37
  13.2 0.7 fusion.32
  14.3 0.6 fusion.27
  15.0 0.7 fusion.25
  15.6 67.5 %while.18 = (s32[]{:T(128)}, f32[1024,256]{1,0:T(8,128)S(1)}, bf16[256,256]{1,0:T(8,128)(2,1)S(1)}, s32[]{:T(128)}, s32[8,2]{0,1:T(2,128)S(1)}, /*index=5*/s32[8...) while((s32[]{:T(128)}, f32[1024,256]{1,0:T(8,128)S(1)}, ...), condition=%wide.region_1.2_spmd.clone, body=%wide.region_0.1_spmd.clone.sunk | while | flops 67633168 | bytes 3024392 | solution.py:55
  15.7 3.0 %collective-permute-start = (bf16[256,256]{1,0:T(8,128)(2,1)S(1)}, bf16[256,256]{1,0:T(8,128)(2,1)S(1)}, u32[]{:S(2)}, u32[]{:S(2)}) collective-permute-start(bf16[256,256]{1,0:T(8,128)(2,1)S(1)} %get-tuple-element.362), channel_id=1, source_target_pairs={{0,4},{4,8},{8,12},{12,16},{16,20},{20,24},{24,28},{28,0},{1,5},{5... | collective-permute-start | bytes 393224 | tf_op jit(solution)/shard_map/while/body/eval_jaxpr/ppermute | solution.py:9
  18.6 0.6 dynamic_slice.114
  19.3 0.7 fusion.54
  20.6 0.6 compare_convert_fusion.3
  22.4 0.6 fusion.56
  23.0 2.2 collective-permute-done
  25.5 0.6 fusion.57
  26.1 0.7 fusion.58
  26.9 0.6 dynamic_slice.114
  27.6 0.7 fusion.54
  28.9 0.6 compare_convert_fusion.3
  30.7 0.6 fusion.56
  31.3 3.3 %collective-permute-done = bf16[256,256]{1,0:T(8,128)(2,1)S(1)} collective-permute-done((bf16[256,256]{1,0:T(8,128)(2,1)S(1)}, bf16[256,256]{1,0:T(8,128)(2,1)S(1)}, u32[]{:S(2)}, u32[]{:S(2)}) %collective-permute-start) | collective-permute-done | bytes 131104 | tf_op jit(solution)/shard_map/while/body/eval_jaxpr/ppermute | solution.py:9
  34.9 0.6 fusion.57
  35.5 0.7 fusion.58
  36.3 0.6 dynamic_slice.114
  36.9 0.7 fusion.54
  38.2 0.6 compare_convert_fusion.3
  40.1 0.6 fusion.56
  40.7 3.3 %collective-permute-done = bf16[256,256]{1,0:T(8,128)(2,1)S(1)} collective-permute-done((bf16[256,256]{1,0:T(8,128)(2,1)S(1)}, bf16[256,256]{1,0:T(8,128)(2,1)S(1)}, u32[]{:S(2)}, u32[]{:S(2)}) %collective-permute-start) | collective-permute-done | bytes 131104 | tf_op jit(solution)/shard_map/while/body/eval_jaxpr/ppermute | solution.py:9
  44.3 0.6 fusion.57
  44.9 0.7 fusion.58
  45.7 0.6 dynamic_slice.114
  46.3 0.7 fusion.54
  47.6 0.6 compare_convert_fusion.3
  49.5 0.6 fusion.56
  50.1 3.3 %collective-permute-done = bf16[256,256]{1,0:T(8,128)(2,1)S(1)} collective-permute-done((bf16[256,256]{1,0:T(8,128)(2,1)S(1)}, bf16[256,256]{1,0:T(8,128)(2,1)S(1)}, u32[]{:S(2)}, u32[]{:S(2)}) %collective-permute-start) | collective-permute-done | bytes 131104 | tf_op jit(solution)/shard_map/while/body/eval_jaxpr/ppermute | solution.py:9
  53.7 0.6 fusion.57
  54.3 0.7 fusion.58
  55.1 0.6 dynamic_slice.114
  55.7 0.7 fusion.54
  57.0 0.6 compare_convert_fusion.3
  59.5 3.3 %collective-permute-done = bf16[256,256]{1,0:T(8,128)(2,1)S(1)} collective-permute-done((bf16[256,256]{1,0:T(8,128)(2,1)S(1)}, bf16[256,256]{1,0:T(8,128)(2,1)S(1)}, u32[]{:S(2)}, u32[]{:S(2)}) %collective-permute-start) | collective-permute-done | bytes 131104 | tf_op jit(solution)/shard_map/while/body/eval_jaxpr/ppermute | solution.py:9
  63.0 0.6 fusion.57
  63.7 0.7 fusion.58
  64.5 0.6 dynamic_slice.114
  65.1 0.7 fusion.54
  66.4 0.6 compare_convert_fusion.3
  68.8 3.3 %collective-permute-done = bf16[256,256]{1,0:T(8,128)(2,1)S(1)} collective-permute-done((bf16[256,256]{1,0:T(8,128)(2,1)S(1)}, bf16[256,256]{1,0:T(8,128)(2,1)S(1)}, u32[]{:S(2)}, u32[]{:S(2)}) %collective-permute-start) | collective-permute-done | bytes 131104 | tf_op jit(solution)/shard_map/while/body/eval_jaxpr/ppermute | solution.py:9
  72.4 0.6 fusion.57
  73.0 0.7 fusion.58
  73.8 0.6 dynamic_slice.114
  74.5 0.7 fusion.54
  75.8 0.6 compare_convert_fusion.3
  78.2 3.3 %collective-permute-done = bf16[256,256]{1,0:T(8,128)(2,1)S(1)} collective-permute-done((bf16[256,256]{1,0:T(8,128)(2,1)S(1)}, bf16[256,256]{1,0:T(8,128)(2,1)S(1)}, u32[]{:S(2)}, u32[]{:S(2)}) %collective-permute-start) | collective-permute-done | bytes 131104 | tf_op jit(solution)/shard_map/while/body/eval_jaxpr/ppermute | solution.py:9
  81.8 0.6 fusion.57
  82.4 0.7 fusion.58
  83.1 0.9 convert_element_type.34
  84.1 19.9 %reduce-scatter.2.cloned.1.call-done = bf16[256,256]{1,0:T(8,128)(2,1)} async-done(((bf16[1024,256]{1,0:T(8,128)(2,1)}), bf16[256,256]{1,0:T(8,128)(2,1)}) %reduce-scatter.2.cloned.1.call-update) | async-done | bytes 131088 | tf_op jit(solution)/shard_map/reduce_scatter | solution.py:56
  104.0 1.8 fusion.38
  105.8 0.9 copy-done.1
  106.8 0.8 fusion.19
  107.6 128.3 %all-reduce.2.cloned.1.call-done = f32[256,256]{1,0:T(8,128)} async-done(((f32[256,256]{1,0:T(8,128)}), f32[256,256]{1,0:T(8,128)}) %all-reduce.2.cloned.1.call-update) | async-done | bytes 262160 | tf_op jit(solution)/shard_map/psum | solution.py:62
  235.9 1.7 broadcast_multiply_fusion
  (64 shorter events, 10.0 us)
Async XLA Ops:
  7.2 96.8 %copy-start = (bf16[256,256]{1,0:T(8,128)(2,1)S(1)}, bf16[256,256]{1,0:T(8,128)(2,1)}, u32[]{:S(2)}) copy-start(bf16[256,256]{1,0:T(8,128)(2,1)} %param.11) | copy-start | bytes 393220
  7.2 96.8 %reduce-scatter.2.cloned.1.call-start = ((), (), s32[]{:S(2)}) async-start(), calls=%async_computation.1 | async-start | bytes 655360 | tf_op jit(solution)/shard_map/reduce_scatter | solution.py:56
  8.2 0.7 copy-start.3
  8.2 2.5 %copy-start.4 = (s32[1,1,8,2,1,256]{5,4,3,2,1,0:T(1,128)S(1)}, s32[1,1,8,2,1,256]{5,4,3,2,1,0:T(1,128)}, u32[]{:S(2)}) copy-start(s32[1,1,8,2,1,256]{5,4,3,2,1,0:T(1,128)} %param.14) | copy-start | bytes 49156
  10.7 0.7 copy-start.5
  15.7 9.5 %collective-permute-start = (bf16[256,256]{1,0:T(8,128)(2,1)S(1)}, bf16[256,256]{1,0:T(8,128)(2,1)S(1)}, u32[]{:S(2)}, u32[]{:S(2)}) collective-permute-start(bf16[256,256]{1,0:T(8,128)(2,1)S(1)} %get-tuple-element.362), channel_id=1, source_target_pairs={{0,4},{4,8},{8,12},{12,16},{16,20},{20,24},{24,28},{28,0},{1,5},{5... | collective-permute-start | bytes 393224 | tf_op jit(solution)/shard_map/while/body/eval_jaxpr/ppermute | solution.py:9
  26.8 7.7 %collective-permute-start = (bf16[256,256]{1,0:T(8,128)(2,1)S(1)}, bf16[256,256]{1,0:T(8,128)(2,1)S(1)}, u32[]{:S(2)}, u32[]{:S(2)}) collective-permute-start(bf16[256,256]{1,0:T(8,128)(2,1)S(1)} %get-tuple-element.362), channel_id=1, source_target_pairs={{0,4},{4,8},{8,12},{12,16},{16,20},{20,24},{24,28},{28,0},{1,5},{5... | collective-permute-start | bytes 393224 | tf_op jit(solution)/shard_map/while/body/eval_jaxpr/ppermute | solution.py:9
  36.2 7.7 %collective-permute-start = (bf16[256,256]{1,0:T(8,128)(2,1)S(1)}, bf16[256,256]{1,0:T(8,128)(2,1)S(1)}, u32[]{:S(2)}, u32[]{:S(2)}) collective-permute-start(bf16[256,256]{1,0:T(8,128)(2,1)S(1)} %get-tuple-element.362), channel_id=1, source_target_pairs={{0,4},{4,8},{8,12},{12,16},{16,20},{20,24},{24,28},{28,0},{1,5},{5... | collective-permute-start | bytes 393224 | tf_op jit(solution)/shard_map/while/body/eval_jaxpr/ppermute | solution.py:9
  45.6 7.7 %collective-permute-start = (bf16[256,256]{1,0:T(8,128)(2,1)S(1)}, bf16[256,256]{1,0:T(8,128)(2,1)S(1)}, u32[]{:S(2)}, u32[]{:S(2)}) collective-permute-start(bf16[256,256]{1,0:T(8,128)(2,1)S(1)} %get-tuple-element.362), channel_id=1, source_target_pairs={{0,4},{4,8},{8,12},{12,16},{16,20},{20,24},{24,28},{28,0},{1,5},{5... | collective-permute-start | bytes 393224 | tf_op jit(solution)/shard_map/while/body/eval_jaxpr/ppermute | solution.py:9
  55.0 7.7 %collective-permute-start = (bf16[256,256]{1,0:T(8,128)(2,1)S(1)}, bf16[256,256]{1,0:T(8,128)(2,1)S(1)}, u32[]{:S(2)}, u32[]{:S(2)}) collective-permute-start(bf16[256,256]{1,0:T(8,128)(2,1)S(1)} %get-tuple-element.362), channel_id=1, source_target_pairs={{0,4},{4,8},{8,12},{12,16},{16,20},{20,24},{24,28},{28,0},{1,5},{5... | collective-permute-start | bytes 393224 | tf_op jit(solution)/shard_map/while/body/eval_jaxpr/ppermute | solution.py:9
  64.4 7.7 %collective-permute-start = (bf16[256,256]{1,0:T(8,128)(2,1)S(1)}, bf16[256,256]{1,0:T(8,128)(2,1)S(1)}, u32[]{:S(2)}, u32[]{:S(2)}) collective-permute-start(bf16[256,256]{1,0:T(8,128)(2,1)S(1)} %get-tuple-element.362), channel_id=1, source_target_pairs={{0,4},{4,8},{8,12},{12,16},{16,20},{20,24},{24,28},{28,0},{1,5},{5... | collective-permute-start | bytes 393224 | tf_op jit(solution)/shard_map/while/body/eval_jaxpr/ppermute | solution.py:9
  73.8 7.7 %collective-permute-start = (bf16[256,256]{1,0:T(8,128)(2,1)S(1)}, bf16[256,256]{1,0:T(8,128)(2,1)S(1)}, u32[]{:S(2)}, u32[]{:S(2)}) collective-permute-start(bf16[256,256]{1,0:T(8,128)(2,1)S(1)} %get-tuple-element.362), channel_id=1, source_target_pairs={{0,4},{4,8},{8,12},{12,16},{16,20},{20,24},{24,28},{28,0},{1,5},{5... | collective-permute-start | bytes 393224 | tf_op jit(solution)/shard_map/while/body/eval_jaxpr/ppermute | solution.py:9
  84.0 151.9 %all-reduce.2.cloned.1.call-start = ((), (), s32[]{:S(2)}) async-start(), calls=%async_computation.2 | async-start | bytes 524288 | tf_op jit(solution)/shard_map/psum | solution.py:62
  105.8 0.9 copy-start.1
  105.8 1.0 copy-start.2
Sparse Core Ops, SparseCore 0:
  84.1 19.7 reduce-scatter.1
  110.9 124.9 all-reduce.1
where the time goes:
time: 245 us; the launch traced here: 244 us
  waiting for transfers between devices  170 us (69%)
  local copies, waits for them, and re-layouts  23.5 us (10%)
  other arithmetic  18 us (7%)
  between operations  15.3 us (6%)
  loops' own time  8.9 us (4%)
  matrix products  5.24 us (2%)
  starting transfers between devices  3.42 us (1%)
    psum x1, waiting for transfers between devices, shards(): total_grad = lax.psum(local_grad, ('blk', 'rep'))  128 us
    ppermute x7, waiting for transfers between devices, shifted(): lax.ppermute(array, axis, [(i, (i + by) % count) for i in range(count)])  21.7 us
    reduce_scatter x1, waiting for transfers between devices, shards(): lax.psum_scatter(totals.astype(jnp.bfloat16), 'rep', scatter_dimension=0,...  19.9 us
    dynamic_update_slice x16, other arithmetic, apply_panel(): lax.dynamic_update_slice_in_dim(totals, current + products[slot] * live_m...  10.5 us
    another operation x1, loops' own time, shards(): totals, _ = lax.fori_loop(1, blocks, cycle_turn, (totals, features))  8.9 us
    broadcast_in_dim x8, local copies, waits for them, and re-layouts, apply_panel(): jnp.where(index_now[..., None] == columns, weight_now[..., None], zero_we...  5.45 us
    convert_element_type x8, other arithmetic, apply_panel(): live_mask = (slot_ids < counts[panel_index]).astype(jnp.float32)  5.04 us
    dynamic_slice x8, local copies, waits for them, and re-layouts, apply_panel(): live_mask = (slot_ids < counts[panel_index]).astype(jnp.float32)  4.95 us
  transfers between devices with their start and end apart: 9, of which 9 were waited for; matrix products, arithmetic and copies ran while one was open for 9% of the time, Pallas kernels for 0%

commit v1 on v0

--- a/solution.py
+++ b/solution.py
@@ -2,6 +2,7 @@
 import jax.numpy as jnp
 from jax import lax
 from jax.sharding import PartitionSpec as P
+from jax.lax import psum
 
 
 def shifted(array, axis, by):
@@ -59,7 +60,7 @@
     local_grad = lax.dot_general(
         summed, pre_cot, (((0,), (0,)), ((), ())), preferred_element_type=jnp.float32
     )
-    total_grad = lax.psum(local_grad, ("blk", "rep"))
+    total_grad = psum(psum(local_grad, "rep"), axis_name="blk")
     node_total = blocks * rep_count * tile_rows
     grad_weight = total_grad * node_total ** (-0.5)
     return (activations, grad_weight)

time: 245 us -> 222 us (0.906)
  waiting for transfers between devices: 170 us -> 147 us
    psum x1 -> x2, waiting for transfers between devices: 128 us -> 105 us  [shards(): total_grad = psum(psum(local_grad, 'rep'), axis_name='blk')]
  transfers between devices with their start and end apart: 9 -> 10, of which waited for: 9 -> 10; matrix products, arithmetic and copies ran while one was open for 9% -> 10% of each run, Pallas kernels for 0% -> 0%
where the time goes in v1:
time: 222 us; the launch traced here: 221 us
  waiting for transfers between devices  147 us (66%)
  local copies, waits for them, and re-layouts  23.5 us (11%)
  other arithmetic  18 us (8%)
  between operations  15 us (7%)
  loops' own time  8.9 us (4%)
  matrix products  5.24 us (2%)
  starting transfers between devices  3.46 us (2%)
    psum x2, waiting for transfers between devices, shards(): total_grad = psum(psum(local_grad, 'rep'), axis_name='blk')  105 us
    ppermute x7, waiting for transfers between devices, shifted(): lax.ppermute(array, axis, [(i, (i + by) % count) for i in range(count)])  21.7 us
    reduce_scatter x1, waiting for transfers between devices, shards(): lax.psum_scatter(totals.astype(jnp.bfloat16), 'rep', scatter_dimension=0,...  19.9 us
    dynamic_update_slice x16, other arithmetic, apply_panel(): lax.dynamic_update_slice_in_dim(totals, current + products[slot] * live_m...  10.5 us
    another operation x1, loops' own time, shards(): totals, _ = lax.fori_loop(1, blocks, cycle_turn, (totals, features))  8.9 us
    broadcast_in_dim x8, local copies, waits for them, and re-layouts, apply_panel(): jnp.where(index_now[..., None] == columns, weight_now[..., None], zero_we...  5.45 us
    convert_element_type x8, other arithmetic, apply_panel(): live_mask = (slot_ids < counts[panel_index]).astype(jnp.float32)  5.04 us
    dynamic_slice x8, local copies, waits for them, and re-layouts, apply_panel(): live_mask = (slot_ids < counts[panel_index]).astype(jnp.float32)  4.95 us
  transfers between devices with their start and end apart: 10, of which 10 were waited for; matrix products, arithmetic and copies ran while one was open for 10% of the time, Pallas kernels for 0%

profile of v1, /device:TPU:0, one launch (start us, length us, event | category | flops | bytes accessed | tf_op | source)
XLA Modules:
  0.0 221.2 jit_solution(8673774227915816582)
XLA Ops:
  7.2 0.9 copy.31
  8.2 0.7 copy-done.3
  10.7 0.6 copy-done.5
  11.4 0.6 constant_dynamic-slice_fusion.3
  12.0 0.6 compare_convert_fusion.1
  12.6 0.6 fusion.37
  13.2 0.7 fusion.32
  14.3 0.6 fusion.27
  15.0 0.7 fusion.25
  15.6 67.5 %while.18 = (s32[]{:T(128)}, f32[1024,256]{1,0:T(8,128)S(1)}, bf16[256,256]{1,0:T(8,128)(2,1)S(1)}, s32[]{:T(128)}, s32[8,2]{0,1:T(2,128)S(1)}, /*index=5*/s32[8...) while((s32[]{:T(128)}, f32[1024,256]{1,0:T(8,128)S(1)}, ...), condition=%wide.region_1.2_spmd.clone, body=%wide.region_0.1_spmd.clone.sunk | while | flops 67633168 | bytes 3024392 | solution.py:56
  15.7 3.0 %collective-permute-start = (bf16[256,256]{1,0:T(8,128)(2,1)S(1)}, bf16[256,256]{1,0:T(8,128)(2,1)S(1)}, u32[]{:S(2)}, u32[]{:S(2)}) collective-permute-start(bf16[256,256]{1,0:T(8,128)(2,1)S(1)} %get-tuple-element.362), channel_id=1, source_target_pairs={{0,4},{4,8},{8,12},{12,16},{16,20},{20,24},{24,28},{28,0},{1,5},{5... | collective-permute-start | bytes 393224 | tf_op jit(solution)/shard_map/while/body/eval_jaxpr/ppermute | solution.py:10
  18.6 0.6 dynamic_slice.114
  19.3 0.7 fusion.54
  20.6 0.6 compare_convert_fusion.3
  22.4 0.6 fusion.56
  23.0 2.2 collective-permute-done
  25.5 0.6 fusion.57
  26.1 0.7 fusion.58
  26.9 0.6 dynamic_slice.114
  27.6 0.7 fusion.54
  28.9 0.6 compare_convert_fusion.3
  30.7 0.6 fusion.56
  31.3 3.3 %collective-permute-done = bf16[256,256]{1,0:T(8,128)(2,1)S(1)} collective-permute-done((bf16[256,256]{1,0:T(8,128)(2,1)S(1)}, bf16[256,256]{1,0:T(8,128)(2,1)S(1)}, u32[]{:S(2)}, u32[]{:S(2)}) %collective-permute-start) | collective-permute-done | bytes 131104 | tf_op jit(solution)/shard_map/while/body/eval_jaxpr/ppermute | solution.py:10
  34.9 0.6 fusion.57
  35.5 0.7 fusion.58
  36.3 0.6 dynamic_slice.114
  36.9 0.7 fusion.54
  38.2 0.6 compare_convert_fusion.3
  40.1 0.6 fusion.56
  40.7 3.3 %collective-permute-done = bf16[256,256]{1,0:T(8,128)(2,1)S(1)} collective-permute-done((bf16[256,256]{1,0:T(8,128)(2,1)S(1)}, bf16[256,256]{1,0:T(8,128)(2,1)S(1)}, u32[]{:S(2)}, u32[]{:S(2)}) %collective-permute-start) | collective-permute-done | bytes 131104 | tf_op jit(solution)/shard_map/while/body/eval_jaxpr/ppermute | solution.py:10
  44.3 0.6 fusion.57
  44.9 0.7 fusion.58
  45.7 0.6 dynamic_slice.114
  46.3 0.7 fusion.54
  47.6 0.6 compare_convert_fusion.3
  50.1 3.3 %collective-permute-done = bf16[256,256]{1,0:T(8,128)(2,1)S(1)} collective-permute-done((bf16[256,256]{1,0:T(8,128)(2,1)S(1)}, bf16[256,256]{1,0:T(8,128)(2,1)S(1)}, u32[]{:S(2)}, u32[]{:S(2)}) %collective-permute-start) | collective-permute-done | bytes 131104 | tf_op jit(solution)/shard_map/while/body/eval_jaxpr/ppermute | solution.py:10
  53.7 0.6 fusion.57
  54.3 0.7 fusion.58
  55.1 0.6 dynamic_slice.114
  55.7 0.7 fusion.54
  57.0 0.6 compare_convert_fusion.3
  59.5 3.3 %collective-permute-done = bf16[256,256]{1,0:T(8,128)(2,1)S(1)} collective-permute-done((bf16[256,256]{1,0:T(8,128)(2,1)S(1)}, bf16[256,256]{1,0:T(8,128)(2,1)S(1)}, u32[]{:S(2)}, u32[]{:S(2)}) %collective-permute-start) | collective-permute-done | bytes 131104 | tf_op jit(solution)/shard_map/while/body/eval_jaxpr/ppermute | solution.py:10
  63.0 0.6 fusion.57
  63.7 0.7 fusion.58
  64.5 0.6 dynamic_slice.114
  65.1 0.7 fusion.54
  66.4 0.6 compare_convert_fusion.3
  68.8 3.3 %collective-permute-done = bf16[256,256]{1,0:T(8,128)(2,1)S(1)} collective-permute-done((bf16[256,256]{1,0:T(8,128)(2,1)S(1)}, bf16[256,256]{1,0:T(8,128)(2,1)S(1)}, u32[]{:S(2)}, u32[]{:S(2)}) %collective-permute-start) | collective-permute-done | bytes 131104 | tf_op jit(solution)/shard_map/while/body/eval_jaxpr/ppermute | solution.py:10
  72.4 0.6 fusion.57
  73.0 0.7 fusion.58
  73.8 0.6 dynamic_slice.114
  74.5 0.7 fusion.54
  75.8 0.6 compare_convert_fusion.3
  78.2 3.3 %collective-permute-done = bf16[256,256]{1,0:T(8,128)(2,1)S(1)} collective-permute-done((bf16[256,256]{1,0:T(8,128)(2,1)S(1)}, bf16[256,256]{1,0:T(8,128)(2,1)S(1)}, u32[]{:S(2)}, u32[]{:S(2)}) %collective-permute-start) | collective-permute-done | bytes 131104 | tf_op jit(solution)/shard_map/while/body/eval_jaxpr/ppermute | solution.py:10
  81.8 0.6 fusion.57
  82.4 0.7 fusion.58
  83.1 0.9 convert_element_type.34
  84.1 19.9 %reduce-scatter.2.cloned.1.call-done = bf16[256,256]{1,0:T(8,128)(2,1)} async-done(((bf16[1024,256]{1,0:T(8,128)(2,1)}), bf16[256,256]{1,0:T(8,128)(2,1)}) %reduce-scatter.2.cloned.1.call-update) | async-done | bytes 131088 | tf_op jit(solution)/shard_map/reduce_scatter | solution.py:57
  104.0 1.8 fusion.38
  105.9 33.1 %all-reduce.3.cloned.1.call-done = f32[256,256]{1,0:T(8,128)} async-done(((f32[256,256]{1,0:T(8,128)}), f32[256,256]{1,0:T(8,128)}) %all-reduce.3.cloned.1.call-update) | async-done | bytes 262160 | tf_op jit(solution)/shard_map/psum | solution.py:63
  139.0 0.9 copy-done.1
  139.9 0.8 fusion.19
  140.8 72.2 %all-reduce.5.cloned.1.call-done = f32[256,256]{1,0:T(8,128)} async-done(((f32[256,256]{1,0:T(8,128)}), f32[256,256]{1,0:T(8,128)}) %all-reduce.5.cloned.1.call-update) | async-done | bytes 262160 | tf_op jit(solution)/shard_map/psum | solution.py:63
  213.0 1.7 broadcast_multiply_fusion
  (67 shorter events, 10.7 us)
Async XLA Ops:
  7.2 96.8 %copy-start = (bf16[256,256]{1,0:T(8,128)(2,1)S(1)}, bf16[256,256]{1,0:T(8,128)(2,1)}, u32[]{:S(2)}) copy-start(bf16[256,256]{1,0:T(8,128)(2,1)} %param.11) | copy-start | bytes 393220
  7.2 96.8 %reduce-scatter.2.cloned.1.call-start = ((), (), s32[]{:S(2)}) async-start(), calls=%async_computation.1 | async-start | bytes 655360 | tf_op jit(solution)/shard_map/reduce_scatter | solution.py:57
  8.2 0.7 copy-start.3
  8.2 2.5 %copy-start.4 = (s32[1,1,8,2,1,256]{5,4,3,2,1,0:T(1,128)S(1)}, s32[1,1,8,2,1,256]{5,4,3,2,1,0:T(1,128)}, u32[]{:S(2)}) copy-start(s32[1,1,8,2,1,256]{5,4,3,2,1,0:T(1,128)} %param.14) | copy-start | bytes 49156
  10.7 0.7 copy-start.5
  15.7 9.5 %collective-permute-start = (bf16[256,256]{1,0:T(8,128)(2,1)S(1)}, bf16[256,256]{1,0:T(8,128)(2,1)S(1)}, u32[]{:S(2)}, u32[]{:S(2)}) collective-permute-start(bf16[256,256]{1,0:T(8,128)(2,1)S(1)} %get-tuple-element.362), channel_id=1, source_target_pairs={{0,4},{4,8},{8,12},{12,16},{16,20},{20,24},{24,28},{28,0},{1,5},{5... | collective-permute-start | bytes 393224 | tf_op jit(solution)/shard_map/while/body/eval_jaxpr/ppermute | solution.py:10
  26.8 7.7 %collective-permute-start = (bf16[256,256]{1,0:T(8,128)(2,1)S(1)}, bf16[256,256]{1,0:T(8,128)(2,1)S(1)}, u32[]{:S(2)}, u32[]{:S(2)}) collective-permute-start(bf16[256,256]{1,0:T(8,128)(2,1)S(1)} %get-tuple-element.362), channel_id=1, source_target_pairs={{0,4},{4,8},{8,12},{12,16},{16,20},{20,24},{24,28},{28,0},{1,5},{5... | collective-permute-start | bytes 393224 | tf_op jit(solution)/shard_map/while/body/eval_jaxpr/ppermute | solution.py:10
  36.2 7.7 %collective-permute-start = (bf16[256,256]{1,0:T(8,128)(2,1)S(1)}, bf16[256,256]{1,0:T(8,128)(2,1)S(1)}, u32[]{:S(2)}, u32[]{:S(2)}) collective-permute-start(bf16[256,256]{1,0:T(8,128)(2,1)S(1)} %get-tuple-element.362), channel_id=1, source_target_pairs={{0,4},{4,8},{8,12},{12,16},{16,20},{20,24},{24,28},{28,0},{1,5},{5... | collective-permute-start | bytes 393224 | tf_op jit(solution)/shard_map/while/body/eval_jaxpr/ppermute | solution.py:10
  45.6 7.7 %collective-permute-start = (bf16[256,256]{1,0:T(8,128)(2,1)S(1)}, bf16[256,256]{1,0:T(8,128)(2,1)S(1)}, u32[]{:S(2)}, u32[]{:S(2)}) collective-permute-start(bf16[256,256]{1,0:T(8,128)(2,1)S(1)} %get-tuple-element.362), channel_id=1, source_target_pairs={{0,4},{4,8},{8,12},{12,16},{16,20},{20,24},{24,28},{28,0},{1,5},{5... | collective-permute-start | bytes 393224 | tf_op jit(solution)/shard_map/while/body/eval_jaxpr/ppermute | solution.py:10
  55.0 7.7 %collective-permute-start = (bf16[256,256]{1,0:T(8,128)(2,1)S(1)}, bf16[256,256]{1,0:T(8,128)(2,1)S(1)}, u32[]{:S(2)}, u32[]{:S(2)}) collective-permute-start(bf16[256,256]{1,0:T(8,128)(2,1)S(1)} %get-tuple-element.362), channel_id=1, source_target_pairs={{0,4},{4,8},{8,12},{12,16},{16,20},{20,24},{24,28},{28,0},{1,5},{5... | collective-permute-start | bytes 393224 | tf_op jit(solution)/shard_map/while/body/eval_jaxpr/ppermute | solution.py:10
  64.4 7.7 %collective-permute-start = (bf16[256,256]{1,0:T(8,128)(2,1)S(1)}, bf16[256,256]{1,0:T(8,128)(2,1)S(1)}, u32[]{:S(2)}, u32[]{:S(2)}) collective-permute-start(bf16[256,256]{1,0:T(8,128)(2,1)S(1)} %get-tuple-element.362), channel_id=1, source_target_pairs={{0,4},{4,8},{8,12},{12,16},{16,20},{20,24},{24,28},{28,0},{1,5},{5... | collective-permute-start | bytes 393224 | tf_op jit(solution)/shard_map/while/body/eval_jaxpr/ppermute | solution.py:10
  73.8 7.7 %collective-permute-start = (bf16[256,256]{1,0:T(8,128)(2,1)S(1)}, bf16[256,256]{1,0:T(8,128)(2,1)S(1)}, u32[]{:S(2)}, u32[]{:S(2)}) collective-permute-start(bf16[256,256]{1,0:T(8,128)(2,1)S(1)} %get-tuple-element.362), channel_id=1, source_target_pairs={{0,4},{4,8},{8,12},{12,16},{16,20},{20,24},{24,28},{28,0},{1,5},{5... | collective-permute-start | bytes 393224 | tf_op jit(solution)/shard_map/while/body/eval_jaxpr/ppermute | solution.py:10
  84.0 55.0 %all-reduce.3.cloned.1.call-start = ((), (), s32[]{:S(2)}) async-start(), calls=%async_computation.2 | async-start | bytes 524288 | tf_op jit(solution)/shard_map/psum | solution.py:63
  105.8 107.1 %all-reduce.5.cloned.1.call-start = ((), (), s32[]{:S(2)}) async-start(), calls=%async_computation.3 | async-start | bytes 524288 | tf_op jit(solution)/shard_map/psum | solution.py:63
  139.0 0.9 copy-start.1
  139.0 1.0 copy-start.2
Sparse Core Ops, SparseCore 0:
  84.1 19.7 reduce-scatter.1
  107.0 31.9 all-reduce.2
  142.3 70.5 all-reduce.4
